TPU v7x, 512 devices: a whole 4x8x8 slice. The times are simulated.
512 devices in a mesh: row: 16 (over y, core), col: 32 (over x, z).
Axes of the slice: x: 4, y: 8, z: 8, core: 2. Of those that a mesh axis runs over, the one named last changes fastest.
Arguments:
- val_waves: bfloat16 [2, 16, 64, 4096], P(None, 'row', 'col'), may hold values from -6 to 6
- cond_waves: bfloat16 [2, 64, 64, 4096], P(None, 'row', 'col'), may hold values from -6 to 6
- val_energy: float32 [16], replicated, may hold values from -6 to -0.5
- cond_energy: float32 [64], replicated, may hold values from 0.5 to 12
- val_index: int32 [512], replicated, may hold values from 0 to 15
- cond_index: int32 [512], replicated, may hold values from 0 to 63
- grid_index: int32 [16384], replicated, may hold values from 0 to 262143, as said below
Outputs:
- chi_zero: float32 [2, 16384, 16384], P(None, 'row', 'col')
Inputs may be any that keep to these rules, and one draw needn't show every extreme that they name: `grid_index`: all entries are different.
All inputs are finite; a program needn't handle non-finite values.
Results may differ from a plain program's by a relative error of at most 0.004.
Values may be sent and summed in bfloat16 or wider, within the bound.
A program may use at most 64 MiB of HBM per device.

v0:
```python
import math

import jax
import jax.numpy as jnp
from jax import lax
from jax.sharding import PartitionSpec as P

GRID = 64
NG = 16384
PAIR_DEV = 32


def spread(value, axis, source):
    kept = jnp.where(lax.axis_index(axis) == source, value, 0).astype(value.dtype)
    return lax.psum(kept, axis)


def dft_tables(length):
    counter = jnp.arange(length, dtype=jnp.int32)
    product = counter[:, None] * counter[None, :] % length
    angles = product.astype(jnp.float32) * (2.0 * math.pi / length)
    return (jnp.cos(angles), jnp.sin(angles))


def middle_transform(field, cosine, sine_table):
    half_width = field.shape[2] // 2
    contract = (((0,), (1,)), ((), ()))
    highest = lax.Precision.HIGHEST
    with_cos = lax.dot_general(cosine, field, contract, precision=highest)
    with_sin = lax.dot_general(sine_table, field, contract, precision=highest)
    rotated = jnp.concatenate([with_sin[..., half_width:], -with_sin[..., :half_width]], axis=-1)
    return with_cos + rotated


def local(val_waves, cond_waves, val_energy, cond_energy, val_index, cond_index, grid_index):
    row_index = lax.axis_index("row")
    col_index = lax.axis_index("col")
    planes = val_waves.shape[2]
    pair_start = row_index * PAIR_DEV
    val_sel = lax.dynamic_slice_in_dim(val_index, pair_start, PAIR_DEV)
    cond_sel = lax.dynamic_slice_in_dim(cond_index, pair_start, PAIR_DEV)
    val_match = val_sel[:, None] == jnp.arange(val_energy.shape[0], dtype=jnp.int32)[None, :]
    cond_match = cond_sel[:, None] == jnp.arange(cond_energy.shape[0], dtype=jnp.int32)[None, :]
    val_level = jnp.sum(jnp.where(val_match, val_energy[None, :], 0.0), axis=1)
    cond_level = jnp.sum(jnp.where(cond_match, cond_energy[None, :], 0.0), axis=1)
    weight = 4.0 / (cond_level - val_level)
    factor = jnp.sqrt(weight) / GRID**1.5
    val_all, cond_all = (
        lax.all_gather(val_waves, "row", axis=1, tiled=True),
        lax.all_gather(cond_waves, "row", axis=1, tiled=True),
    )
    valence = jnp.take(val_all, val_sel, axis=1).astype(jnp.float32)
    conduction = jnp.take(cond_all, cond_sel, axis=1).astype(jnp.float32)
    dens_real = (valence[0] * conduction[0] + valence[1] * conduction[1]) * factor[:, None, None]
    dens_imag = (valence[0] * conduction[1] - valence[1] * conduction[0]) * factor[:, None, None]
    cosine, sine_table = dft_tables(GRID)
    columns = 2 * PAIR_DEV * planes
    stacked = jnp.stack([dens_real, dens_imag], axis=0).reshape(columns, GRID * GRID)
    field = jnp.transpose(stacked).reshape(GRID, GRID, columns)
    field = middle_transform(field, cosine, sine_table)
    field = middle_transform(field, cosine, sine_table)
    table = field.reshape(GRID * GRID, columns)
    position = col_index * planes + jnp.arange(planes, dtype=jnp.int32)
    owned_rows = NG // (2 * lax.axis_size("col"))
    freq_x = grid_index // (GRID * GRID)
    inner_spot = grid_index % (GRID * GRID)
    picked = jnp.take(table, inner_spot, axis=0).reshape(
        2 * (owned_rows * lax.axis_size("col")), 2, PAIR_DEV, planes
    )
    phase = (freq_x[:, None] * position[None, :] % GRID).astype(jnp.float32) * (
        2.0 * math.pi / GRID
    )
    phase_cos = jnp.cos(phase)[:, None, None, :]
    phase_sin = jnp.sin(phase)[:, None, None, :]
    sum_cos = jnp.sum(picked * phase_cos, axis=3)
    sum_sin = jnp.sum(picked * phase_sin, axis=3)
    total_real = sum_cos[:, 0] + sum_sin[:, 1]
    total_imag = sum_cos[:, 1] - sum_sin[:, 0]
    summed = lax.psum_scatter(
        jnp.stack([total_real, total_imag], axis=1).reshape(
            owned_rows * lax.axis_size("col"), 4 * PAIR_DEV
        ),
        "col",
        scatter_dimension=0,
        tiled=True,
    )
    spectrum = summed.reshape(2 * owned_rows, 2, PAIR_DEV)
    amplitude = spectrum.astype(jnp.bfloat16)
    col_factor = lax.all_gather(amplitude, "row", axis=2, tiled=True)
    ratio = lax.axis_size("col") // lax.axis_size("row")
    pieces = []
    for block_number in range(ratio):
        pieces.append(spread(col_factor, "col", row_index * ratio + block_number))
    row_factor = jnp.concatenate(pieces, axis=0)
    pair_total = col_factor.shape[2]
    row_count_all = row_factor.shape[0]
    left_side = row_factor.reshape(row_count_all, 2 * pair_total)
    swapped = jnp.concatenate([row_factor[:, 1], -row_factor[:, 0]], axis=1)
    left_both = jnp.concatenate([left_side, swapped], axis=0)
    right_side = col_factor.reshape(col_factor.shape[0], 2 * pair_total)
    contract = (((1,), (1,)), ((), ()))
    scale_out = -1.0 / pair_total
    product = (
        lax.dot_general(left_both, right_side, contract, preferred_element_type=jnp.float32)
        * scale_out
    )
    return product.reshape(2, row_count_all, right_side.shape[0])


def solution(mesh):
    placed = (P(None, "row", "col", None), P(None, "row", "col", None), P(), P(), P(), P(), P())
    return jax.shard_map(
        local, mesh=mesh, in_specs=placed, out_specs=P(None, "row", "col"), check_vma=False
    )
```

profile of v0, /device:TPU:1, one launch (start us, length us, event | category | flops | bytes accessed | tf_op | source)
XLA Modules:
  0.0 679.3 jit_solution(17896875043684915092)
XLA Ops:
  9.4 1.2 compare_and_fusion.1
  13.0 22.7 %all_gather.9 = bf16[2,16,2,4096]{3,2,1,0:T(2,128)(2,1)S(1)} all-gather(bf16[2,1,2,4096]{3,2,1,0:T(2,128)(2,1)} %param.7), channel_id=1, replica_groups=mesh['row'=16,'col'=32] {'row'}, dimensions={1}, use_global_device_ids=true | all-gather | bytes 557056 | tf_op jit(solution)/shard_map/all_gather | solution.py:49
  36.2 2.7 gather_fusion
  38.9 1.0 convert_bitcast_fusion.1
  40.0 2.4 fusion.19
  42.4 14.8 %all-gather.3.cloned.1.call-done = bf16[2,64,2,4096]{3,2,1,0:T(2,128)(2,1)} async-done(((bf16[2,4,2,4096]{3,2,1,0:T(2,128)(2,1)}), bf16[2,64,2,4096]{3,2,1,0:T(2,128)(2,1)}) %all-gather.3.cloned.1.call-update) | async-done | bytes 2097168 | tf_op jit(solution)/shard_map/all_gather | solution.py:50
  57.2 4.4 gather_fusion.1
  61.6 1.6 convert_bitcast_fusion
  63.2 1.9 add_multiply_fusion
  65.1 1.8 pad_maximum_fusion.1
  67.2 2.4 reshape.120
  69.6 2.1 copy.47
  71.7 2.1 fusion.27
  74.6 2.6 maximum_add_fusion
  77.3 3.1 fusion.9
  81.2 3.8 maximum_add_fusion.1
  85.1 1.2 copy.50
  86.3 54.8 %gather_fusion.2 = f32[16384,128]{1,0:T(8,128)} fusion(f32[4096,128]{1,0:T(8,128)S(1)} %bitcast.30, s32[16384]{0:T(1024)S(1)} %get-tuple-element.28), kind=kCustom, calls=%fused_computation.2 | custom fusion | bytes 16842752 | tf_op jit(solution)/shard_map/jit(_take)/gather | solution.py:67
  141.1 9.0 %copy.51 = f32[16384,128]{0,1:T(8,128)} copy(f32[16384,128]{1,0:T(8,128)} %gather_fusion.2) | data formatting | bytes 16777216 | tf_op jit(solution)/shard_map/jit(_take)/gather | solution.py:67
  150.1 10.6 %gather.17 = f32[16384,2,32,2]{0,3,2,1:T(2,128)} reshape(f32[16384,128]{0,1:T(8,128)} %copy.51) | data formatting | bytes 16777216 | tf_op jit(solution)/shard_map/jit(_take)/gather | solution.py:67
  160.6 25.2 %multiply_reduce_fusion.1 = (f32[16384,2,32]{0,2,1:T(8,128)S(1)}, f32[16384,2,32]{0,2,1:T(8,128)}) fusion(f32[16384,2,32,2]{0,3,2,1:T(2,128)} %gather.17, pred[16384]{0:T(1024)(128)(4,1)S(1)} %compare_and_fusion, f32[16384,2]{0,1:T(2,128)S(1)} %get-tuple-element.26, f32[16384,2]{0,1:T(2,128)S(1)} %get-tuple-element.25), kind=kLoop, calls=%fused_computation.4 | loop fusion | flops 8388608 | bytes 17055744 | tf_op jit(solution)/shard_map/reduce_sum | solution.py:75
  185.8 2.8 slice_add_fusion
  188.5 2.3 pad_maximum_fusion
  190.9 19.4 %copy.52 = f32[16384,2,32]{2,1,0:T(2,128)} copy(f32[16384,2,32]{0,2,1:T(8,128)} %pad_maximum_fusion) | data formatting | bytes 8388608 | tf_op jit(solution)/shard_map/stack | solution.py:80
  210.3 16.7 %reshape.123 = f32[8192,128]{1,0:T(8,128)} reshape(f32[16384,2,32]{2,1,0:T(2,128)} %copy.52) | data formatting | bytes 8388608 | tf_op jit(solution)/shard_map/reshape | solution.py:80
  227.1 221.1 %reduce-scatter.2.cloned.1.call-done = f32[256,128]{1,0:T(8,128)} async-done(((f32[8192,128]{1,0:T(8,128)}), f32[256,128]{1,0:T(8,128)}) %reduce-scatter.2.cloned.1.call-update) | async-done | bytes 131088 | tf_op jit(solution)/shard_map/reduce_scatter | solution.py:79
  450.1 44.4 %all-gather.5.cloned.1.call-done = bf16[512,2,512]{0,1,2:T(2,128)(2,1)} async-done(((bf16[512,2,32]{0,1,2:T(2,128)(2,1)}), bf16[512,2,512]{0,1,2:T(2,128)(2,1)}) %all-gather.5.cloned.1.call-update) | async-done | bytes 1048592 | tf_op jit(solution)/shard_map/all_gather | solution.py:89
  494.6 2.7 copy.54
  497.3 1.5 broadcast_select_fusion.3
  499.0 160.5 %all-reduce.3.cloned.1.call-done = (bf16[512,2,512]{2,0,1:T(8,128)(2,1)}, bf16[512,2,512]{2,0,1:T(8,128)(2,1)}) async-done(((bf16[512,2,512]{2,0,1:T(8,128)(2,1)}, bf16[512,2,512]{2,0,1:T(8,128)(2,1)}), (bf16[512,2,512]{2,0,1:T(8,128)(2,1)}, bf16[512,2,512]{2,0,1:T(8,128)(2,1)})) %all-reduce.3.cloned.1.call-update) | async-done | bytes 2097168 | tf_op jit(solution)/shard_map/psum | solution.py:15
  659.5 1.4 constant_dynamic-update-slice_fusion.1
  661.6 10.7 %fusion.6 = f32[2048,512]{1,0:T(8,128)} fusion(bf16[512,1024]{0,1:T(8,128)(2,1)S(1)} %bitcast.36, bf16[1024,512]{1,0:T(8,128)(2,1)S(1)} %get-tuple-element.18, bf16[1024,512]{1,0:T(8,128)(2,1)S(1)} %get-tuple-element.17, bf16[1024,1024]{1,0:T(8,128)(2,1)S(1)} %bitcast.35), kind=kOutput, calls=%fused_computation.13 | convolution fusion | flops 2161115136 | bytes 9437184 | tf_op jit(solution)/shard_map/dot_general | solution.py:104
  (39 shorter events, 10.6 us)
Async XLA Ops:
  6.5 50.7 %all-gather.3.cloned.1.call-start = ((), (), s32[]{:S(2)}) async-start(), calls=%async_computation.1 | async-start | bytes 2228224 | tf_op jit(solution)/shard_map/all_gather | solution.py:50
  7.3 441.0 %reduce-scatter.2.cloned.1.call-start = ((), (), s32[]{:S(2)}) async-start(), calls=%async_computation.2 | async-start | bytes 4325376 | tf_op jit(solution)/shard_map/reduce_scatter | solution.py:79
  38.9 1.0 copy-start.2
  38.9 1.1 copy-start.3
  61.6 1.6 copy-start.4
  227.0 267.6 %all-gather.5.cloned.1.call-start = ((), (), s32[]{:S(2)}) async-start(), calls=%async_computation.3 | async-start | bytes 1114112 | tf_op jit(solution)/shard_map/all_gather | solution.py:89
  450.1 209.5 %all-reduce.3.cloned.1.call-start = ((), (), s32[]{:S(2)}) async-start(), calls=%async_computation.4 | async-start | bytes 4194304 | tf_op jit(solution)/shard_map/psum | solution.py:15
  497.3 1.6 copy-start
  659.5 1.5 copy-start.1
Sparse Core Ops, SparseCore 0:
  9.5 47.6 all-gather.2
  227.1 221.0 reduce-scatter.1
  450.6 43.9 all-gather.4
  498.9 160.5 all-reduce.2
where the time goes:
time: 691 us; the launch traced here: 679 us
  waiting for transfers between devices  442 us (64%)
  local copies, waits for them, and re-layouts  129 us (19%)
  other arithmetic  49.4 us (7%)
  blocking collectives  22.7 us (3%)
  matrix products  22.3 us (3%)
  between operations  13.8 us (2%)
    reduce_scatter x1, waiting for transfers between devices, local(): lax.psum_scatter(jnp.stack([total_real, total_imag], axis=1).reshape(owne...  221 us
    psum x1, waiting for transfers between devices, spread(): return lax.psum(kept, axis)  161 us
    gather x3, local copies, waits for them, and re-layouts, local(): jnp.take(table, inner_spot, axis=0)  74.3 us
    all_gather x1, waiting for transfers between devices, local(): col_factor = lax.all_gather(amplitude, 'row', axis=2, tiled=True)  44.4 us
    reduce_sum x1, other arithmetic, local(): sum_cos = jnp.sum(picked * phase_cos, axis=3)  25.2 us
    all_gather x1, blocking collectives, local(): lax.all_gather(val_waves, 'row', axis=1, tiled=True)  22.7 us
    another operation x1, local copies, waits for them, and re-layouts, local(): jnp.stack([total_real, total_imag], axis=1)  19.4 us
    reshape x1, local copies, waits for them, and re-layouts, local(): jnp.stack([total_real, total_imag], axis=1)  16.7 us
  transfers between devices with their start and end apart: 4, of which 4 were waited for; matrix products, arithmetic and copies ran while one was open for 2% of the time, Pallas kernels for 0%

commit v1 on v0

v1 whole, which is shorter than its diff:
```python
import functools
import math

import jax
import jax.numpy as jnp
import numpy as np
from jax import lax
from jax.experimental import pallas as pl
from jax.experimental.pallas import tpu as pltpu
from jax.sharding import PartitionSpec as P

GRID = 64
ROWS = 16
COLS = 32
CHIPS_Y = 8
CHIPS_X = 4
CHIPS_Z = 8
BANDS_DEV = 5
VMEM = pl.BlockSpec(memory_space=pltpu.VMEM)
SMEM = pl.BlockSpec(memory_space=pltpu.SMEM)
MESH = pl.DeviceIdType.MESH
VMEM_LIMIT = 56 * 1024 * 1024


def remote(src, dst, send, recv, **where):
    return pltpu.make_async_remote_copy(
        src_ref=src, dst_ref=dst, send_sem=send, recv_sem=recv,
        device_id=where, device_id_type=MESH,
    )


def greet(peers):
    barrier = pltpu.get_barrier_semaphore()
    for where in peers:
        pl.semaphore_signal(barrier, inc=1, device_id=where, device_id_type=MESH)
    pl.semaphore_wait(barrier, len(peers))


class RowGather:
    def __init__(self, own, buffer, send, recv):
        r = lax.axis_index("row")
        self.y, self.core = r // 2, r % 2
        self.own, self.buffer, self.send, self.recv = own, buffer, send, recv

    def slot(self, step, core=None):
        y = lax.rem(self.y + step + CHIPS_Y, CHIPS_Y)
        return y * 2 + (self.core if core is None else core)

    def copy(self, number, step, target):
        at = self.slot(step)
        src = self.own if step == 0 else self.buffer.at[at]
        return remote(src, self.buffer.at[at], self.send.at[number], self.recv.at[number], row=target)

    def right(self, step):
        return self.copy(step, -step, self.slot(1))

    def left(self, step):
        return self.copy(4 + step, step, self.slot(-1))

    def mate(self, step):
        return self.copy(7 + (step % CHIPS_Y), step, self.slot(0, 1 - self.core))

    def start(self):
        self.right(0).start()
        self.left(0).start()
        self.mate(0).start()

    def turn(self, step):
        self.right(step - 1).wait_recv()
        if step < 4:
            self.right(step).start()
        self.mate(-step).start()
        if step < 4:
            self.left(step - 1).wait_recv()
            if step < 3:
                self.left(step).start()
            self.mate(step).start()

    def finish(self):
        for step in range(-4, 4):
            self.mate(step).wait()
        for step in range(4):
            self.right(step).wait_send()
        for step in range(3):
            self.left(step).wait_send()


def density_kernel(val_slot, cond_slot, factor, own, out, bands, staged, ring_send, ring_recv, send, recv):
    r, c = lax.axis_index("row"), lax.axis_index("col")
    y, core = r // 2, r % 2
    row_peers = [
        lax.rem(y + 1, CHIPS_Y) * 2 + core, lax.rem(y + CHIPS_Y - 1, CHIPS_Y) * 2 + core, y * 2 + 1 - core
    ]
    greet([{"row": p} for p in row_peers] + [{"col": lax.rem(c + k, COLS)} for k in range(1, COLS)])
    gather = RowGather(own, bands, ring_send, ring_recv)
    gather.start()
    bands[r] = own[...]
    for step in range(1, 5):
        gather.turn(step)
    gather.finish()

    lane = lax.broadcasted_iota(jnp.int32, (128, 128), 1)

    def density(pair):
        bra = bands[val_slot[pair, 0], 0].astype(jnp.float32)
        ket = bands[cond_slot[pair, 0], cond_slot[pair, 1]].astype(jnp.float32)
        same = bra * ket
        cross = bra * pltpu.roll(ket, 64, 1)
        real = same + pltpu.roll(same, 64, 1)
        imag = pltpu.roll(cross, 64, 1) - cross
        return (jnp.where(lane < 64, real, imag) * factor[pair]).astype(jnp.bfloat16)

    def push(k):
        to = lax.rem(c + k, COLS)
        return remote(staged.at[to], out.at[c], send.at[k], recv.at[k], col=to)

    def produce(k, _):
        to = lax.rem(c + k, COLS)
        staged[to] = density(to)
        push(k).start()
        return 0

    lax.fori_loop(1, COLS, produce, 0)
    out[c] = density(c)

    def settle(k, _):
        origin = lax.rem(c - k + COLS, COLS)
        remote(staged.at[origin], out.at[origin], send.at[k], recv.at[k], col=origin).wait_recv()
        push(k).wait_send()
        return 0

    lax.fori_loop(1, COLS, settle, 0)


def pair_densities(val_slot, cond_slot, factor, own):
    return pl.pallas_call(
        density_kernel,
        out_shape=jax.ShapeDtypeStruct((COLS, 128, 128), jnp.bfloat16),
        in_specs=[SMEM, SMEM, SMEM, VMEM],
        out_specs=VMEM,
        scratch_shapes=[
            pltpu.VMEM((ROWS, BANDS_DEV, 128, 128), jnp.bfloat16),
            pltpu.VMEM((COLS, 128, 128), jnp.bfloat16),
            pltpu.SemaphoreType.DMA((15,)),
            pltpu.SemaphoreType.DMA((15,)),
            pltpu.SemaphoreType.DMA((COLS,)),
            pltpu.SemaphoreType.DMA((COLS,)),
        ],
        compiler_params=pltpu.CompilerParams(
            collective_id=0, has_side_effects=True, vmem_limit_bytes=VMEM_LIMIT
        ),
        name="pair_densities",
    )(val_slot, cond_slot, factor, own)


def tables():
    angle = 2.0 * math.pi / GRID * (np.outer(np.arange(GRID), np.arange(GRID)) % GRID)
    cos, sin = np.cos(angle), np.sin(angle)

    def split(table):
        high = table.astype(jnp.bfloat16)
        low = (table - high.astype(np.float64)).astype(jnp.bfloat16)
        return high, low

    z_high, z_low = split(np.block([[cos, -sin], [sin, cos]]))
    left_high, left_low = split(np.concatenate([cos, sin], axis=0))
    z_table = np.concatenate([z_high, z_low], axis=0)
    left_table = np.concatenate([left_high, left_low, left_high], axis=1)
    return jnp.asarray(z_table), jnp.asarray(left_table)


def spectrum_kernel(dens, z_table, left_table, index, amp_rows, amp_cols, first, second, picked, block):
    z_tab = z_table[...]
    left_tab = left_table[...]
    sign = jnp.where(lax.broadcasted_iota(jnp.int32, (64, 128), 1) < 64, 1.0, -1.0)

    def along_z(i, _):
        part = dens[pl.ds(i * 4, 4)].reshape(512, 128)
        wide = jnp.concatenate([part, part], axis=1)
        first[pl.ds(pl.multiple_of(i * 512, 512), 512), :] = jnp.dot(
            wide, z_tab, preferred_element_type=jnp.float32
        )
        return 0

    lax.fori_loop(0, 8, along_z, 0)

    def transform(parts):
        high = [p.astype(jnp.bfloat16) for p in parts]
        low = [(p - h.astype(jnp.float32)).astype(jnp.bfloat16) for p, h in zip(parts, high)]
        high = jnp.concatenate(high, axis=1)
        low = jnp.concatenate(low, axis=1)
        got = jnp.dot(
            left_tab, jnp.concatenate([high, high, low], axis=0), preferred_element_type=jnp.float32
        )
        return [
            got[:64, 128 * n : 128 * (n + 1)]
            + sign * pltpu.roll(got[64:, 128 * n : 128 * (n + 1)], 64, 1)
            for n in range(len(parts))
        ]

    def along_y(i, _):
        base = pl.multiple_of(i * 512, 512)
        parts = [first[pl.ds(base + 64 * n, 64), :] for n in range(8)]
        for n, part in enumerate(transform(parts)):
            second[pl.ds(base + 64 * n, 64), :] = part
        return 0

    lax.fori_loop(0, 8, along_y, 0)

    for i in range(8):
        parts = [second[pl.ds(i * 8 + n, 64, stride=64), :] for n in range(8)]
        done = transform(parts)
        for n in range(4):
            tile = jnp.concatenate(done[2 * n : 2 * n + 2], axis=0)
            number = i * 4 + n
            picked[
                pl.ds((number // 8) * 128, 128), pl.ds((number % 8) * 128, 128)
            ] = tile.T.astype(jnp.bfloat16)

    inner = lax.broadcasted_iota(jnp.int32, (1024, 1024), 0)
    outer = lax.broadcasted_iota(jnp.int32, (256, 1024), 0)

    def select(t, _):
        spot = index[pl.ds(t, 1), :]
        kx, ky, kz = spot // 4096, (spot // 64) % 64, spot % 64
        hot = jnp.where(inner == (ky % 16) * 64 + kx, 1.0, 0.0).astype(jnp.bfloat16)
        got = jnp.dot(picked[...], hot, preferred_element_type=jnp.float32)
        keep = outer == (ky // 16) * 64 + kz
        for part in range(2):
            half = jnp.concatenate(
                [got[128 * g + 64 * part : 128 * g + 64 * part + 64] for g in range(4)], axis=0
            )
            row = jnp.sum(jnp.where(keep, half, 0.0), axis=0, keepdims=True)
            for j in range(8):
                piece = row[:, 128 * j : 128 * (j + 1)]
                block[pl.ds(8 * part + j, 1), :] = piece
                amp_cols[2 * t + j // 4, pl.ds(4 * part + j % 4, 1), :] = piece
        amp_rows[t] = block[...].astype(jnp.bfloat16)
        return 0

    lax.fori_loop(0, 16, select, 0)


def spectrum(dens, index):
    z_table, left_table = tables()
    return pl.pallas_call(
        spectrum_kernel,
        out_shape=(
            jax.ShapeDtypeStruct((ROWS, 16, 128), jnp.bfloat16),
            jax.ShapeDtypeStruct((COLS, 8, 128), jnp.float32),
        ),
        in_specs=[VMEM] * 4,
        out_specs=(VMEM, VMEM),
        scratch_shapes=[
            pltpu.VMEM((4096, 128), jnp.float32),
            pltpu.VMEM((4096, 128), jnp.float32),
            pltpu.VMEM((512, 1024), jnp.bfloat16),
            pltpu.VMEM((16, 128), jnp.float32),
        ],
        compiler_params=pltpu.CompilerParams(vmem_limit_bytes=VMEM_LIMIT),
        name="spectrum",
    )(dens, z_table, left_table, index.reshape(16, 1024))


def exchange_kernel(
    amp_rows, amp_cols, left, right,
    row_land, row_wide, col_land, row_send, row_recv, col_send, col_recv,
    c_send, c_recv, a_send, a_recv, b_send, b_recv,
):
    r, c = lax.axis_index("row"), lax.axis_index("col")
    x, z = c // CHIPS_Z, c % CHIPS_Z
    greet(
        [{"row": lax.rem(r + k, ROWS)} for k in range(1, ROWS)]
        + [{"col": lax.rem(c + k, COLS)} for k in range(1, COLS)]
    )

    def row_push(k):
        to = lax.rem(r + k, ROWS)
        return remote(amp_rows.at[to], row_land.at[r], row_send.at[k], row_recv.at[k], row=to)

    def col_push(k):
        to = lax.rem(c + k, COLS)
        return remote(
            amp_cols.at[to], col_land.at[pl.ds(pl.multiple_of(c * 8, 8), 8)],
            col_send.at[k], col_recv.at[k], col=to,
        )

    def row_begin(k, _):
        row_push(k).start()
        return 0

    def col_begin(k, _):
        col_push(k).start()
        return 0

    lax.fori_loop(1, ROWS, row_begin, 0)
    lax.fori_loop(1, COLS, col_begin, 0)
    row_land[r] = amp_rows[r]
    col_land[pl.ds(pl.multiple_of(c * 8, 8), 8), :] = amp_cols[c]

    def row_settle(k, _):
        origin = lax.rem(r - k + ROWS, ROWS)
        remote(
            amp_rows.at[origin], row_land.at[origin], row_send.at[k], row_recv.at[k], row=origin
        ).wait_recv()
        return 0

    def col_settle(k, _):
        origin = lax.rem(c - k + COLS, COLS)
        remote(
            amp_cols.at[origin], col_land.at[pl.ds(pl.multiple_of(origin * 8, 8), 8)],
            col_send.at[k], col_recv.at[k], col=origin,
        ).wait_recv()
        return 0

    lax.fori_loop(1, ROWS, row_settle, 0)
    row_wide[...] = row_land[...].astype(jnp.float32).reshape(256, 128)
    for j in range(16):
        left[x, z, j] = row_wide[pl.ds(j, 16, stride=16), :].astype(jnp.bfloat16)

    def x_at(step):
        return lax.rem(x + step + CHIPS_X, CHIPS_X)

    def z_at(step):
        return lax.rem(z + step + CHIPS_Z, CHIPS_Z)

    def a_z(number, step, toward):
        ref = left.at[x, z_at(step), pl.ds(0, 8)]
        return remote(ref, ref, a_send.at[number], a_recv.at[number], col=x * CHIPS_Z + z_at(toward))

    def a_right(step):
        return a_z(step, -step, 1)

    def a_left(step):
        return a_z(4 + step, step, -1)

    def a_x(number, step, toward, low, count):
        ref = left.at[x_at(step), pl.ds(low, count), pl.ds(0, 8)]
        return remote(ref, ref, a_send.at[number], a_recv.at[number], col=x_at(toward) * CHIPS_Z + z)

    def b_x(number, toward):
        ref = left.at[x, z, pl.ds(8, 8)]
        return remote(ref, ref, b_send.at[number], b_recv.at[number], col=x_at(toward) * CHIPS_Z + z)

    def b_z(number, step, toward):
        ref = left.at[:, z_at(step), pl.ds(8, 8)]
        return remote(ref, ref, b_send.at[number], b_recv.at[number], col=x * CHIPS_Z + z_at(toward))

    def b_right(step):
        return b_z(step, -step, 1)

    def b_left(step):
        return b_z(4 + step, step, -1)

    for number, toward in ((7, 1), (8, -1), (9, 2)):
        b_x(number, toward).start()
    a_right(0).start()
    a_left(0).start()

    lax.fori_loop(1, COLS, col_settle, 0)
    for q in range(8):
        right[r, q] = col_land[pl.ds(q, 32, stride=8), :].astype(jnp.bfloat16)
    gather = RowGather(right.at[r], right, c_send, c_recv)
    gather.start()

    for number, toward in ((7, 1), (8, -1), (9, 2)):
        b_x(number, toward).wait_recv()
    b_right(0).start()
    b_left(0).start()
    for step in range(1, 5):
        a_right(step - 1).wait_recv()
        if step < 4:
            a_right(step).start()
            a_left(step - 1).wait_recv()
            if step < 3:
                a_left(step).start()
        if step < 4:
            gather.turn(step)
    across = [a_x(7, 0, 1, 0, 8), a_x(8, 0, -1, 0, 8), a_x(9, -1, 1, 0, 4), a_x(10, 1, -1, 4, 4)]
    across[0].start()
    across[1].start()
    gather.turn(4)
    for step in range(1, 5):
        b_right(step - 1).wait_recv()
        if step < 4:
            b_right(step).start()
            b_left(step - 1).wait_recv()
            if step < 3:
                b_left(step).start()
        if step == 2:
            across[0].wait_recv()
            across[2].start()
            across[1].wait_recv()
            across[3].start()
    across[2].wait_recv()
    across[3].wait_recv()

    gather.finish()
    for step in range(4):
        a_right(step).wait_send()
        b_right(step).wait_send()
    for step in range(3):
        a_left(step).wait_send()
        b_left(step).wait_send()
    for number, toward in ((7, 1), (8, -1), (9, 2)):
        b_x(number, toward).wait_send()
    for copy in across:
        copy.wait_send()

    def row_end(k, _):
        row_push(k).wait_send()
        return 0

    def col_end(k, _):
        col_push(k).wait_send()
        return 0

    lax.fori_loop(1, ROWS, row_end, 0)
    lax.fori_loop(1, COLS, col_end, 0)


def exchange(amp_rows, amp_cols):
    dma = pltpu.SemaphoreType.DMA
    return pl.pallas_call(
        exchange_kernel,
        out_shape=(
            jax.ShapeDtypeStruct((CHIPS_X, CHIPS_Z, 16, 16, 128), jnp.bfloat16),
            jax.ShapeDtypeStruct((ROWS, 8, 32, 128), jnp.bfloat16),
        ),
        in_specs=[VMEM, VMEM],
        out_specs=(VMEM, VMEM),
        scratch_shapes=[
            pltpu.VMEM((ROWS, 16, 128), jnp.bfloat16),
            pltpu.VMEM((256, 128), jnp.float32),
            pltpu.VMEM((256, 128), jnp.float32),
            dma((ROWS,)), dma((ROWS,)), dma((COLS,)), dma((COLS,)),
            dma((15,)), dma((15,)), dma((11,)), dma((11,)), dma((10,)), dma((10,)),
        ],
        compiler_params=pltpu.CompilerParams(
            collective_id=1, has_side_effects=True, vmem_limit_bytes=VMEM_LIMIT
        ),
        name="exchange",
    )(amp_rows, amp_cols)


def product_kernel(left, right, out, wide, rhs):
    @pl.when(pl.program_id(0) == 0)
    def _():
        wide[...] = right[...].reshape(4096, 128).astype(jnp.float32)

        def reorder(c, _):
            for q in range(8):
                rhs[
                    pl.ds(pl.multiple_of((q // 4) * 512 + c * 16, 16), 16), pl.ds((q % 4) * 128, 128)
                ] = wide[pl.ds(q * 32 + c, 16, stride=256), :].astype(jnp.bfloat16)
            return 0

        lax.fori_loop(0, COLS, reorder, 0)

    real = left[:, pl.program_id(0)].reshape(512, 128)
    imag = left[:, 8 + pl.program_id(0)].reshape(512, 128)
    lhs = jnp.concatenate(
        [jnp.concatenate([real, imag], axis=0), jnp.concatenate([imag, -real], axis=0)], axis=1
    )
    got = lax.dot_general(
        lhs, rhs[...], (((0,), (0,)), ((), ())), preferred_element_type=jnp.float32
    ) * (-1.0 / 512)
    out[0] = got[:128]
    out[1] = got[128:]


def product(left, right):
    return pl.pallas_call(
        product_kernel,
        grid=(8,),
        out_shape=jax.ShapeDtypeStruct((2, 1024, 512), jnp.float32),
        in_specs=[VMEM, VMEM],
        out_specs=pl.BlockSpec((2, 128, 512), lambda j: (0, j, 0)),
        scratch_shapes=[pltpu.VMEM((4096, 128), jnp.float32), pltpu.VMEM((1024, 512), jnp.bfloat16)],
        compiler_params=pltpu.CompilerParams(vmem_limit_bytes=VMEM_LIMIT),
        name="product",
    )(left.reshape(COLS, 16, 16, 128), right)


def local(val_waves, cond_waves, val_energy, cond_energy, val_index, cond_index, grid_index):
    pair_start = lax.axis_index("row") * COLS
    val_sel = lax.dynamic_slice_in_dim(val_index, pair_start, COLS)
    cond_sel = lax.dynamic_slice_in_dim(cond_index, pair_start, COLS)
    val_match = val_sel[:, None] == jnp.arange(val_energy.shape[0], dtype=jnp.int32)[None, :]
    cond_match = cond_sel[:, None] == jnp.arange(cond_energy.shape[0], dtype=jnp.int32)[None, :]
    val_level = jnp.sum(jnp.where(val_match, val_energy[None, :], 0.0), axis=1)
    cond_level = jnp.sum(jnp.where(cond_match, cond_energy[None, :], 0.0), axis=1)
    factor = jnp.sqrt(4.0 / (cond_level - val_level)) / GRID**1.5
    waves = jnp.concatenate([val_waves, cond_waves], axis=1).reshape(2, BANDS_DEV, 2, GRID, GRID)
    own = jnp.transpose(waves, (1, 2, 3, 0, 4)).reshape(BANDS_DEV, 128, 128)
    val_slot = jnp.stack([val_sel, val_sel * 0], axis=1)
    cond_slot = jnp.stack([cond_sel // 4, cond_sel % 4 + 1], axis=1)
    dens = pair_densities(val_slot, cond_slot, factor, own)
    amp_rows, amp_cols = spectrum(dens, grid_index)
    left, right = exchange(amp_rows, amp_cols)
    return product(left, right)


def solution(mesh):
    placed = (P(None, "row", "col", None), P(None, "row", "col", None), P(), P(), P(), P(), P())
    return jax.shard_map(
        local, mesh=mesh, in_specs=placed, out_specs=P(None, "row", "col"), check_vma=False
    )
```

time: 691 us -> 162 us (0.23); the launches traced: 679 us -> 159 us
  waiting for transfers between devices: 442 us -> 0 us
  Pallas kernels: 0 us -> 150 us
  local copies, waits for them, and re-layouts: 129 us -> 5.78 us
  other arithmetic: 49.4 us -> 4.08 us
  blocking collectives: 22.7 us -> 0 us
  matrix products: 22.3 us -> 0 us
  between operations: 13.8 us -> 0.04 us
    reduce_scatter x1 -> x0, waiting for transfers between devices: 221 us -> none  [local(): lax.psum_scatter(jnp.stack([total_real, total_imag], axis=1).reshape(owne...]
    psum x1 -> x0, waiting for transfers between devices: 161 us -> none  [spread(): return lax.psum(kept, axis)]
    pallas_call x0 -> x4, Pallas kernels: none -> 150 us  [the longest x1 66.4 us: pair_densities(): pl.pallas_call(density_kernel, out_shape=jax.ShapeDtypeStruct((COLS, 128,...]
    gather x5 -> x0, local copies, waits for them, and re-layouts: 81.3 us -> none  [the longest x3 74.3 us: local(): jnp.take(table, inner_spot, axis=0)]
    all_gather x2 -> x0, waiting for transfers between devices: 59.2 us -> none  [the longest x1 44.4 us: local(): col_factor = lax.all_gather(amplitude, 'row', axis=2, tiled=True)]
    reduce_sum x1 -> x0, other arithmetic: 25.2 us -> none  [local(): sum_cos = jnp.sum(picked * phase_cos, axis=3)]
    all_gather x1 -> x0, blocking collectives: 22.7 us -> none  [local(): lax.all_gather(val_waves, 'row', axis=1, tiled=True)]
    dot_general x5 -> x0, matrix products: 22.3 us -> none  [the longest x1 10.7 us: local(): lax.dot_general(left_both, right_side, contract, preferred_element_type=j...]
  transfers between devices with their start and end apart: 4 -> 0, of which waited for: 4 -> 0; matrix products, arithmetic and copies ran while one was open for 2% -> 0% of each run, Pallas kernels for 0% -> 0%
where the time goes in v1:
time: 162 us; the launch traced here: 159 us
  Pallas kernels  150 us (93%)
  local copies, waits for them, and re-layouts  5.78 us (4%)
  other arithmetic  4.08 us (3%)
    pallas_call x1, Pallas kernels, pair_densities(): pl.pallas_call(density_kernel, out_shape=jax.ShapeDtypeStruct((COLS, 128,...  66.4 us
    pallas_call x1, Pallas kernels, exchange(): pl.pallas_call(exchange_kernel, out_shape=(jax.ShapeDtypeStruct((CHIPS_X,...  42.3 us
    pallas_call x1, Pallas kernels, spectrum(): pl.pallas_call(spectrum_kernel, out_shape=(jax.ShapeDtypeStruct((ROWS, 16...  30.9 us
    pallas_call x1, Pallas kernels, product(): pl.pallas_call(product_kernel, grid=(8,), out_shape=jax.ShapeDtypeStruct(...  9.98 us

profile of v1, /device:TPU:1, one launch (start us, length us, event | category | flops | bytes accessed | tf_op | source)
XLA Modules:
  0.0 159.4 jit_solution(5622244885672362309)
XLA Ops:
  0.0 0.8 dynamic-slice_bitcast_fusion
  0.8 0.8 dynamic_slice.6
  1.5 0.7 select_reduce_fusion.1
  2.3 0.8 fusion.2
  3.0 0.8 select_reduce_fusion
  3.9 0.6 sqrt_multiply_fusion.factor
  4.5 0.7 copy.19.cond_slot
  5.2 0.1 copy.17
  5.2 0.6 stack.17.val_slot
  5.9 1.5 reshape.18.index
  7.3 1.1 pad_maximum_fusion
  8.5 0.2 reshape.16
  8.7 0.3 copy.21
  9.0 0.8 reshape.17.own
  9.9 66.4 %pair_densities.1.dens = bf16[32,128,128]{2,1,0:T(8,128)(2,1)} custom-call(s32[32,2]{1,0:T(8,128)} %stack.17.val_slot, s32[32,2]{1,0:T(8,128)} %copy.19.cond_slot, f32[32]{0:T(128)} %sqrt_multiply_fusion.factor, bf16[5,128,128]{2,1,0:T(8,128)(2,1)} %reshape.17.own), custom_call_target="tpu_custom_call" | custom-call | tf_op jit(solution)/shard_map/pair_densities/pallas_call | solution.py:136
  76.3 30.9 %spectrum.1 = (bf16[16,16,128]{2,1,0:T(8,128)(2,1)}, f32[32,8,128]{2,1,0:T(8,128)}) custom-call(bf16[32,128,128]{2,1,0:T(8,128)(2,1)} %pair_densities.1.dens, bf16[256,128]{1,0:T(8,128)(2,1)} %constant.52.clone.z_table, bf16[128,192]{1,0:T(8,128)(2,1)} %constant.53.clone.left_table, s32[16,1024]{1,0:T(8,128)} %reshape.18.index), custom_call_target="tpu_custom_call" | custom-call | tf_op jit(solution)/shard_map/spectrum/pallas_call | solution.py:246
  107.1 42.3 %exchange.1 = (bf16[4,8,16,16,128]{4,3,2,1,0:T(8,128)(2,1)}, bf16[16,8,32,128]{3,2,1,0:T(8,128)(2,1)}) custom-call(bf16[16,16,128]{2,1,0:T(8,128)(2,1)} %get-tuple-element.9.amp_rows, f32[32,8,128]{2,1,0:T(8,128)} %get-tuple-element.10.amp_cols), custom_call_target="tpu_custom_call" | custom-call | tf_op jit(solution)/shard_map/exchange/pallas_call | solution.py:424
  149.4 10.0 %product.1 = f32[2,1024,512]{2,1,0:T(8,128)} custom-call(bf16[32,16,16,128]{3,2,1,0:T(8,128)(2,1)} %bitcast.10, bf16[16,8,32,128]{3,2,1,0:T(8,128)(2,1)} %get-tuple-element.12.right), custom_call_target="tpu_custom_call" | custom-call | tf_op jit(solution)/shard_map/product/pallas_call | solution.py:473
  (2 shorter events, 0.0 us)

commit v2 on v0

v2 whole, which is shorter than its diff:
```python
import math

import jax
import jax.numpy as jnp
import numpy as np
from jax import lax
from jax.experimental import pallas as pl
from jax.experimental.pallas import tpu as pltpu
from jax.sharding import PartitionSpec as P

GRID = 64
ROWS = 16
COLS = 32
CHIPS_Y = 8
CHIPS_X = 4
CHIPS_Z = 8
BANDS_DEV = 5
VMEM = pl.BlockSpec(memory_space=pltpu.VMEM)
SMEM = pl.BlockSpec(memory_space=pltpu.SMEM)
MESH = pl.DeviceIdType.MESH
VMEM_LIMIT = 56 * 1024 * 1024
CHUNKS = 4
CHUNK = 128 // CHUNKS


def remote(src, dst, send, recv, **where):
    return pltpu.make_async_remote_copy(
        src_ref=src, dst_ref=dst, send_sem=send, recv_sem=recv,
        device_id=where, device_id_type=MESH,
    )


def shifted(value, step, size):
    return lax.rem(value + step + size, size)


class RowGather:
    MATES = {0: 7, -1: 8, -2: 9, 1: 10, 2: 11, -3: 12, -4: 13, 3: 14}

    def __init__(self, view, send, recv):
        r = lax.axis_index("row")
        self.y, self.core = r // 2, r % 2
        self.view, self.send, self.recv = view, send, recv

    def copy(self, number, block, toward):
        ref = self.view(shifted(self.y, block, CHIPS_Y) * 2 + self.core)
        target = shifted(self.y, toward, CHIPS_Y) * 2 + self.core
        return remote(ref, ref, self.send(number), self.recv(number), row=target)

    def mate(self, block):
        ref = self.view(shifted(self.y, block, CHIPS_Y) * 2 + self.core)
        number = self.MATES[block]
        return remote(ref, ref, self.send(number), self.recv(number), row=self.y * 2 + 1 - self.core)

    def hop(self, number):
        block, toward = ((0, 1), (0, 2), (0, -1), (0, -2), (-2, 1), (-2, 2), (2, -1))[number]
        return self.copy(number, block, toward)

    def start(self):
        for number in (0, 2, 1, 3):
            self.hop(number).start()
        self.mate(0).start()

    def middle(self):
        self.hop(1).wait_recv()
        self.hop(4).start()
        self.hop(5).start()
        self.hop(3).wait_recv()
        self.hop(6).start()
        self.hop(0).wait_recv()
        self.hop(2).wait_recv()
        for block in (-1, 1, -2, 2):
            self.mate(block).start()

    def end(self):
        for number, block in ((4, -3), (6, 3), (5, -4)):
            self.hop(number).wait_recv()
            self.mate(block).start()
        for block in self.MATES:
            self.mate(block).wait_recv()

    def finish(self):
        for number in range(7):
            self.hop(number).wait_send()
        for block in self.MATES:
            self.mate(block).wait_send()


class ColGather:
    Z_STEPS = (1, -1, 2, -2, 3, -3, 4)
    X_STEPS = (1, -1, 2)

    def __init__(self, view, send, recv):
        c = lax.axis_index("col")
        self.x, self.z = c // CHIPS_Z, c % CHIPS_Z
        self.view, self.send, self.recv = view, send, recv

    def along_z(self, i):
        ref = self.view(self.x, self.z)
        target = self.x * CHIPS_Z + shifted(self.z, self.Z_STEPS[i], CHIPS_Z)
        return remote(ref, ref, self.send(i), self.recv(i), col=target)

    def along_x(self, i, j):
        block = self.z if i == 0 else shifted(self.z, -self.Z_STEPS[i - 1], CHIPS_Z)
        ref = self.view(self.x, block)
        number = 7 + 3 * i + j
        target = shifted(self.x, self.X_STEPS[j], CHIPS_X) * CHIPS_Z + self.z
        return remote(ref, ref, self.send(number), self.recv(number), col=target)

    def spread(self, i):
        for j in range(3):
            self.along_x(i, j).start()

    def start(self):
        for i in range(7):
            self.along_z(i).start()
        self.spread(0)

    def forward(self, i):
        self.along_z(i).wait_recv()
        self.spread(i + 1)

    def arrive(self):
        for i in range(8):
            for j in range(3):
                self.along_x(i, j).wait_recv()

    def finish(self):
        for i in range(7):
            self.along_z(i).wait_send()
        for i in range(8):
            for j in range(3):
                self.along_x(i, j).wait_send()


def tables():
    angle = 2.0 * math.pi / GRID * (np.outer(np.arange(GRID), np.arange(GRID)) % GRID)
    cos, sin = np.cos(angle), np.sin(angle)

    def split(table):
        high = table.astype(jnp.bfloat16)
        low = (table - high.astype(np.float64)).astype(jnp.bfloat16)
        return high, low

    z_high, z_low = split(np.block([[cos, -sin], [sin, cos]]))
    left_high, left_low = split(np.concatenate([cos, sin], axis=0))
    z_table = np.concatenate([z_high, z_low], axis=0)
    left_table = np.concatenate([left_high, left_low, left_high], axis=1)
    return jnp.asarray(z_table), jnp.asarray(left_table)


def window_kernel(
    val_index, cond_index, val_energy, cond_energy, own, z_table, left_table, index,
    left, rhs,
    bands_0, bands_1, bands_2, bands_3, staged, dens, first, second, picked, amp, row_land, col_land, right, wide,
    band_send, band_recv, pair_send, pair_recv, row_send, row_recv, col_send, col_recv,
    left_send, left_recv, right_send, right_recv,
):
    r, c = lax.axis_index("row"), lax.axis_index("col")
    x, z = c // CHIPS_Z, c % CHIPS_Z
    barrier = pltpu.get_barrier_semaphore()
    for k in range(1, ROWS):
        pl.semaphore_signal(barrier, inc=1, device_id={"row": lax.rem(r + k, ROWS)}, device_id_type=MESH)
    for k in range(1, COLS):
        pl.semaphore_signal(barrier, inc=1, device_id={"col": lax.rem(c + k, COLS)}, device_id_type=MESH)
    bands = (bands_0, bands_1, bands_2, bands_3)
    for q in range(CHUNKS):
        bands[q][r] = own[:, pl.ds(CHUNK * q, CHUNK)]
    pl.semaphore_wait(barrier, ROWS + COLS - 2)

    lane = lax.broadcasted_iota(jnp.int32, (CHUNK, 128), 1)

    def band_part(q):
        return RowGather(
            lambda slot: bands[q].at[slot],
            lambda n: band_send.at[q, n],
            lambda n: band_recv.at[q, n],
        )

    def density(pair, q):
        v, w = val_index[r * COLS + pair], cond_index[r * COLS + pair]
        bra = bands[q][v, 0].astype(jnp.float32)
        ket = bands[q][w // 4, 1 + w % 4].astype(jnp.float32)
        gap = jnp.full((CHUNK, 128), cond_energy[w] - val_energy[v], jnp.float32)
        factor = jnp.sqrt(4.0 / gap) * (1.0 / 512)
        same = bra * ket
        cross = bra * pltpu.roll(ket, 64, 1)
        real = same + pltpu.roll(same, 64, 1)
        imag = pltpu.roll(cross, 64, 1) - cross
        return (jnp.where(lane < 64, real, imag) * factor).astype(jnp.bfloat16)

    def pair_copy(k, q):
        to = lax.rem(c + k, COLS)
        rows = pl.ds(CHUNK * q, CHUNK)
        return remote(
            staged.at[to, rows], dens.at[c, rows], pair_send.at[q, k], pair_recv.at[q, k], col=to
        )

    def pair_part(q):
        def step(k, _):
            to = lax.rem(c + k, COLS)
            staged[to, pl.ds(CHUNK * q, CHUNK)] = density(to, q)
            pair_copy(k, q).start()
            return 0

        lax.fori_loop(1, COLS, step, 0)
        dens[c, pl.ds(CHUNK * q, CHUNK)] = density(c, q)

    parts = [band_part(q) for q in range(CHUNKS)]
    parts[0].start()
    if CHUNKS > 1:
        parts[1].start()
    parts[0].middle()
    for q in range(CHUNKS):
        if q + 2 < CHUNKS:
            parts[q + 2].start()
        if q + 1 < CHUNKS:
            parts[q + 1].middle()
        parts[q].end()
        pair_part(q)

    z_tab = z_table[...]
    left_tab = left_table[...]
    sign = jnp.where(lax.broadcasted_iota(jnp.int32, (64, 128), 1) < 64, 1.0, -1.0)

    def transform(parts):
        high = [p.astype(jnp.bfloat16) for p in parts]
        low = [(p - h.astype(jnp.float32)).astype(jnp.bfloat16) for p, h in zip(parts, high)]
        high = jnp.concatenate(high, axis=1)
        low = jnp.concatenate(low, axis=1)
        got = jnp.dot(
            left_tab, jnp.concatenate([high, high, low], axis=0), preferred_element_type=jnp.float32
        )
        return [
            got[:64, 128 * n : 128 * (n + 1)]
            + sign * pltpu.roll(got[64:, 128 * n : 128 * (n + 1)], 64, 1)
            for n in range(len(parts))
        ]

    for q in range(CHUNKS):
        def arrived(k, _):
            origin = lax.rem(c - k + COLS, COLS)
            rows = pl.ds(CHUNK * q, CHUNK)
            remote(
                staged.at[origin, rows], dens.at[origin, rows], pair_send.at[q, k], pair_recv.at[q, k],
                col=origin,
            ).wait_recv()
            return 0

        lax.fori_loop(1, COLS, arrived, 0)
        part = dens[:, pl.ds(CHUNK * q, CHUNK)].reshape(COLS * CHUNK, 128)
        got = jnp.dot(
            jnp.concatenate([part, part], axis=1), z_tab, preferred_element_type=jnp.float32
        )
        first[:, pl.ds(CHUNK * q, CHUNK)] = got.reshape(COLS, CHUNK, 128)
        if (q + 1) * CHUNK % 64 == 0:
            plane = (q + 1) * CHUNK // 64 - 1

            def along_y(i, _):
                got = transform([first[i * 8 + n, pl.ds(64 * plane, 64)] for n in range(8)])
                for n in range(8):
                    base = pl.multiple_of((i * 8 + n) * 128 + 64 * plane, 64)
                    second[pl.ds(base, 64), :] = got[n]
                return 0

            lax.fori_loop(0, 4, along_y, 0)

    for i in range(8):
        done = transform([second[pl.ds(i * 8 + n, 64, stride=64), :] for n in range(8)])
        for n in range(4):
            tile = jnp.concatenate(done[2 * n : 2 * n + 2], axis=0)
            number = i * 4 + n
            picked[
                pl.ds((number // 8) * 128, 128), pl.ds((number % 8) * 128, 128)
            ] = tile.T.astype(jnp.bfloat16)

    inner = lax.broadcasted_iota(jnp.int32, (1024, 1024), 0)
    outer = lax.broadcasted_iota(jnp.int32, (256, 1024), 0)

    def row_copy(b, h, rr):
        return remote(amp.at[b], row_land.at[h, r], row_send.at[b], row_recv.at[h, r], row=rr)

    def col_copy(b):
        return remote(amp.at[b], col_land.at[c], col_send.at[b], col_recv.at[c], col=b)

    def select(h):
        def step(t, _):
            blocks = (4 * t + h, 4 * t + 2 + h)
            spot = jnp.concatenate(
                [index[pl.ds(4 * b + i, 1), :] for b in blocks for i in range(4)], axis=1
            )
            kx, ky, kz = spot // 4096, (spot // 64) % 64, spot % 64
            hot = jnp.where(inner == (ky % 16) * 64 + kx, 1.0, 0.0).astype(jnp.bfloat16)
            got = jnp.dot(picked[...], hot, preferred_element_type=jnp.float32)
            keep = outer == (ky // 16) * 64 + kz
            for part in range(2):
                half = jnp.concatenate(
                    [got[128 * g + 64 * part : 128 * g + 64 * part + 64] for g in range(4)], axis=0
                )
                row = jnp.sum(jnp.where(keep, half, 0.0), axis=0, keepdims=True)
                for j in range(8):
                    amp[blocks[j // 4], pl.ds(4 * part + j % 4, 1), :] = row[:, 128 * j : 128 * (j + 1)]
            for n, b in enumerate(blocks):
                rr = 2 * t + n

                @pl.when(rr != r)
                def _():
                    row_copy(b, h, rr).start()

                @pl.when(rr == r)
                def _():
                    row_land[h, r] = amp[b]

                @pl.when(b != c)
                def _():
                    col_copy(b).start()

                @pl.when(b == c)
                def _():
                    col_land[c] = amp[b]
            return 0

        return step

    def row_half(h):
        def settle(k, _):
            origin = lax.rem(r - k + ROWS, ROWS)
            remote(
                amp.at[0], row_land.at[h, origin], row_send.at[0], row_recv.at[h, origin], row=origin
            ).wait_recv()
            return 0

        lax.fori_loop(1, ROWS, settle, 0)
        wide[pl.ds(0, 128), :] = row_land[h].reshape(128, 128)
        for j in range(8):
            left[h, x, z, j] = wide[pl.ds(j, 16, stride=8), :].astype(jnp.bfloat16)
        return ColGather(
            lambda xx, zz: left.at[h, xx, zz], lambda n: left_send.at[h, n], lambda n: left_recv.at[h, n]
        )

    lax.fori_loop(0, 8, select(0), 0)
    early = row_half(0)
    early.start()
    for low, high, ready in ((0, 2, (0, 1)), (2, 4, (2, 3)), (4, 6, (4, 5, 6)), (6, 8, ())):
        lax.fori_loop(low, high, select(1), 0)
        for i in ready:
            early.forward(i)
    late = row_half(1)
    late.start()

    def col_settle(k, _):
        origin = lax.rem(c - k + COLS, COLS)
        remote(
            amp.at[0], col_land.at[origin], col_send.at[0], col_recv.at[origin], col=origin
        ).wait_recv()
        return 0

    lax.fori_loop(1, COLS, col_settle, 0)
    wide[pl.ds(0, 256), :] = col_land[...].reshape(256, 128)
    for j in range(8):
        right[r, j] = wide[pl.ds(j, 32, stride=8), :].astype(jnp.bfloat16)
    column = RowGather(lambda slot: right.at[slot], lambda n: right_send.at[n], lambda n: right_recv.at[n])
    column.start()
    for i in range(4):
        late.forward(i)
    column.middle()
    for i in range(4, 7):
        late.forward(i)
    column.end()

    wide[...] = right[...].reshape(4096, 128).astype(jnp.float32)

    def reorder(n, _):
        for q in range(8):
            rhs[
                pl.ds(pl.multiple_of((q // 4) * 512 + n * 16, 16), 16), pl.ds((q % 4) * 128, 128)
            ] = wide[pl.ds(q * 32 + n, 16, stride=256), :].astype(jnp.bfloat16)
        return 0

    lax.fori_loop(0, COLS, reorder, 0)

    for part in parts:
        part.finish()

    def pair_end(k, _):
        for q in range(CHUNKS):
            pair_copy(k, q).wait_send()
        return 0

    lax.fori_loop(1, COLS, pair_end, 0)

    def amp_end(b, _):
        @pl.when(b // 2 != r)
        def _():
            row_copy(b, b % 2, b // 2).wait_send()

        @pl.when(b != c)
        def _():
            col_copy(b).wait_send()

        return 0

    lax.fori_loop(0, COLS, amp_end, 0)
    early.arrive()
    late.arrive()
    early.finish()
    late.finish()
    column.finish()


def window(val_index, cond_index, val_energy, cond_energy, own, index):
    z_table, left_table = tables()
    dma = pltpu.SemaphoreType.DMA
    f32, bf16 = jnp.float32, jnp.bfloat16
    return pl.pallas_call(
        window_kernel,
        out_shape=(
            jax.ShapeDtypeStruct((2, CHIPS_X, CHIPS_Z, 8, 16, 128), bf16),
            jax.ShapeDtypeStruct((1024, 512), bf16),
        ),
        in_specs=[SMEM] * 4 + [VMEM] * 4,
        out_specs=(VMEM, VMEM),
        scratch_shapes=[
            *[pltpu.VMEM((ROWS, BANDS_DEV, CHUNK, 128), bf16) for _ in range(CHUNKS)],
            pltpu.VMEM((COLS, 128, 128), bf16),
            pltpu.VMEM((COLS, 128, 128), bf16),
            pltpu.VMEM((COLS, 128, 128), f32),
            pltpu.VMEM((4096, 128), f32),
            pltpu.VMEM((512, 1024), bf16),
            pltpu.VMEM((COLS, 8, 128), f32),
            pltpu.VMEM((2, ROWS, 8, 128), f32),
            pltpu.VMEM((COLS, 8, 128), f32),
            pltpu.VMEM((ROWS, 8, COLS, 128), bf16),
            pltpu.VMEM((4096, 128), f32),
            dma((CHUNKS, 15)), dma((CHUNKS, 15)), dma((CHUNKS, COLS)), dma((CHUNKS, COLS)),
            dma((COLS,)), dma((2, ROWS)), dma((COLS,)), dma((COLS,)),
            dma((2, 31)), dma((2, 31)), dma((15,)), dma((15,)),
        ],
        compiler_params=pltpu.CompilerParams(
            collective_id=0, has_side_effects=True, vmem_limit_bytes=VMEM_LIMIT
        ),
        name="window",
    )(val_index, cond_index, val_energy, cond_energy, own, z_table, left_table, index)


def product_kernel(real, imag, rhs, out):
    real = real[...].reshape(512, 128)
    imag = imag[...].reshape(512, 128)
    lhs = jnp.concatenate(
        [jnp.concatenate([real, imag], axis=0), jnp.concatenate([imag, -real], axis=0)], axis=1
    )
    got = lax.dot_general(
        lhs, rhs[...], (((0,), (0,)), ((), ())), preferred_element_type=jnp.float32
    ) * (-1.0 / 512)
    out[0] = got[:128]
    out[1] = got[128:]


def product(left, rhs):
    block = (1, CHIPS_X, CHIPS_Z, 1, 16, 128)
    return pl.pallas_call(
        product_kernel,
        grid=(8,),
        out_shape=jax.ShapeDtypeStruct((2, 1024, 512), jnp.float32),
        in_specs=[
            pl.BlockSpec(block, lambda j: (j // 4, 0, 0, j % 4, 0, 0)),
            pl.BlockSpec(block, lambda j: (j // 4, 0, 0, j % 4 + 4, 0, 0)),
            VMEM,
        ],
        out_specs=pl.BlockSpec((2, 128, 512), lambda j: (0, j, 0)),
        compiler_params=pltpu.CompilerParams(vmem_limit_bytes=VMEM_LIMIT),
        name="product",
    )(left, left, rhs)


def local(val_waves, cond_waves, val_energy, cond_energy, val_index, cond_index, grid_index):
    waves = jnp.concatenate([val_waves, cond_waves], axis=1).reshape(2, BANDS_DEV, 2, GRID, GRID)
    own = jnp.transpose(waves, (1, 2, 3, 0, 4)).reshape(BANDS_DEV, 128, 128)
    left, rhs = window(
        val_index, cond_index, val_energy, cond_energy, own, grid_index.reshape(128, 128)
    )
    return product(left, rhs)


def solution(mesh):
    placed = (P(None, "row", "col", None), P(None, "row", "col", None), P(), P(), P(), P(), P())
    return jax.shard_map(
        local, mesh=mesh, in_specs=placed, out_specs=P(None, "row", "col"), check_vma=False
    )
```

time: 691 us -> 128 us (0.19); the launches traced: 679 us -> 127 us
  waiting for transfers between devices: 442 us -> 0 us
  local copies, waits for them, and re-layouts: 129 us -> 1.42 us
  Pallas kernels: 0 us -> 124 us
  other arithmetic: 49.4 us -> 1.12 us
  blocking collectives: 22.7 us -> 0 us
  matrix products: 22.3 us -> 0 us
  between operations: 13.8 us -> 0.03 us
    reduce_scatter x1 -> x0, waiting for transfers between devices: 221 us -> none  [local(): lax.psum_scatter(jnp.stack([total_real, total_imag], axis=1).reshape(owne...]
    psum x1 -> x0, waiting for transfers between devices: 161 us -> none  [spread(): return lax.psum(kept, axis)]
    pallas_call x0 -> x2, Pallas kernels: none -> 124 us  [the longest x1 116 us: window(): pl.pallas_call(window_kernel, out_shape=(jax.ShapeDtypeStruct((2, CHIPS_X...]
    gather x5 -> x0, local copies, waits for them, and re-layouts: 81.3 us -> none  [the longest x3 74.3 us: local(): jnp.take(table, inner_spot, axis=0)]
    all_gather x2 -> x0, waiting for transfers between devices: 59.2 us -> none  [the longest x1 44.4 us: local(): col_factor = lax.all_gather(amplitude, 'row', axis=2, tiled=True)]
    reduce_sum x3 -> x0, other arithmetic: 26.8 us -> none  [the longest x1 25.2 us: local(): sum_cos = jnp.sum(picked * phase_cos, axis=3)]
    all_gather x1 -> x0, blocking collectives: 22.7 us -> none  [local(): lax.all_gather(val_waves, 'row', axis=1, tiled=True)]
    dot_general x5 -> x0, matrix products: 22.3 us -> none  [the longest x1 10.7 us: local(): lax.dot_general(left_both, right_side, contract, preferred_element_type=j...]
  transfers between devices with their start and end apart: 4 -> 0, of which waited for: 4 -> 0; matrix products, arithmetic and copies ran while one was open for 2% -> 0% of each run, Pallas kernels for 0% -> 0%
where the time goes in v2:
time: 128 us; the launch traced here: 127 us
  Pallas kernels  124 us (97%)
  local copies, waits for them, and re-layouts  1.42 us (1%)
    pallas_call x1, Pallas kernels, window(): pl.pallas_call(window_kernel, out_shape=(jax.ShapeDtypeStruct((2, CHIPS_X...  116 us
    pallas_call x1, Pallas kernels, product(): pl.pallas_call(product_kernel, grid=(8,), out_shape=jax.ShapeDtypeStruct(...  8.25 us

profile of v2, /device:TPU:1, one launch (start us, length us, event | category | flops | bytes accessed | tf_op | source)
XLA Modules:
  0.0 127.0 jit_solution(10208808941168472284)
XLA Ops:
  0.0 1.1 pad_maximum_fusion
  1.1 0.2 reshape.9
  1.4 0.3 copy.12
  1.7 0.8 reshape.10.own
  2.6 116.2 %window.1 = (bf16[2,4,8,8,16,128]{5,4,3,2,1,0:T(8,128)(2,1)}, bf16[1024,512]{1,0:T(8,128)(2,1)}) custom-call(s32[512]{0:T(512)} %val_index.1, s32[512]{0:T(512)} %cond_index.1, f32[16]{0:T(128)} %val_energy.1, f32[64]{0:T(128)} %cond_energy.1, bf16[5,128,128]{2,1,0:T(8,128)(2,1)} %reshape.10.own, bf16[256,128]{1,0:T(8,128)(2,1)} %constant.4.clone.z_table, ...), custom_call_target="tpu_custom_call" | custom-call | tf_op jit(solution)/shard_map/window/pallas_call | solution.py:415
  118.8 8.2 %product.1 = f32[2,1024,512]{2,1,0:T(8,128)} custom-call(bf16[2,4,8,8,16,128]{5,4,3,2,1,0:T(8,128)(2,1)} %get-tuple-element.7.real.imag, bf16[2,4,8,8,16,128]{5,4,3,2,1,0:T(8,128)(2,1)} %get-tuple-element.7.real.imag, bf16[1024,512]{1,0:T(8,128)(2,1)} %get-tuple-element.8.rhs), custom_call_target="tpu_custom_call" | custom-call | tf_op jit(solution)/shard_map/product/pallas_call | solution.py:461

commit v3 on v2

--- a/solution.py
+++ b/solution.py
@@ -19,8 +19,9 @@
 SMEM = pl.BlockSpec(memory_space=pltpu.SMEM)
 MESH = pl.DeviceIdType.MESH
 VMEM_LIMIT = 56 * 1024 * 1024
-CHUNKS = 4
-CHUNK = 128 // CHUNKS
+SLAB = 16
+GROUP = 8
+Y_STEPS = (1, -1, 2, -2, 3, -3, 4)
 
 
 def remote(src, dst, send, recv, **where):
@@ -152,72 +153,91 @@
 def window_kernel(
     val_index, cond_index, val_energy, cond_energy, own, z_table, left_table, index,
     left, rhs,
-    bands_0, bands_1, bands_2, bands_3, staged, dens, first, second, picked, amp, row_land, col_land, right, wide,
+    bands, staged, dens, first, second, picked, amp, row_land, col_land, right, wide,
     band_send, band_recv, pair_send, pair_recv, row_send, row_recv, col_send, col_recv,
     left_send, left_recv, right_send, right_recv,
 ):
     r, c = lax.axis_index("row"), lax.axis_index("col")
     x, z = c // CHIPS_Z, c % CHIPS_Z
+    y, core = r // 2, r % 2
+    def slab(chip):
+        return pl.ds(pl.multiple_of(chip * SLAB, SLAB), SLAB)
+
     barrier = pltpu.get_barrier_semaphore()
     for k in range(1, ROWS):
         pl.semaphore_signal(barrier, inc=1, device_id={"row": lax.rem(r + k, ROWS)}, device_id_type=MESH)
     for k in range(1, COLS):
         pl.semaphore_signal(barrier, inc=1, device_id={"col": lax.rem(c + k, COLS)}, device_id_type=MESH)
-    bands = (bands_0, bands_1, bands_2, bands_3)
-    for q in range(CHUNKS):
-        bands[q][r] = own[:, pl.ds(CHUNK * q, CHUNK)]
+    bands[r] = own[:, slab(y)]
     pl.semaphore_wait(barrier, ROWS + COLS - 2)
 
-    lane = lax.broadcasted_iota(jnp.int32, (CHUNK, 128), 1)
-
-    def band_part(q):
-        return RowGather(
-            lambda slot: bands[q].at[slot],
-            lambda n: band_send.at[q, n],
-            lambda n: band_recv.at[q, n],
+    def band_push(i):
+        chip = shifted(y, Y_STEPS[i], CHIPS_Y)
+        return remote(
+            own.at[:, slab(chip)], bands.at[r], band_send.at[i], band_recv.at[i], row=chip * 2 + core
         )
 
-    def density(pair, q):
-        v, w = val_index[r * COLS + pair], cond_index[r * COLS + pair]
-        bra = bands[q][v, 0].astype(jnp.float32)
-        ket = bands[q][w // 4, 1 + w % 4].astype(jnp.float32)
-        gap = jnp.full((CHUNK, 128), cond_energy[w] - val_energy[v], jnp.float32)
+    def band_mate(i):
+        ref = bands.at[r if i == 7 else shifted(y, -Y_STEPS[i], CHIPS_Y) * 2 + core]
+        return remote(ref, ref, band_send.at[8 + i], band_recv.at[8 + i], row=y * 2 + 1 - core)
+
+    for i in range(7):
+        band_push(i).start()
+    band_mate(7).start()
+    for i in range(7):
+        band_push(i).wait_recv()
+        band_mate(i).start()
+    for i in range(8):
+        band_mate(i).wait_recv()
+
+    lane = lax.broadcasted_iota(jnp.int32, (SLAB, 128), 1)
+
+    def density(pair):
+        v, w = val_index[pair], cond_index[pair]
+        bra = bands[v, 0].astype(jnp.float32)
+        ket = bands[w // 4, 1 + w % 4].astype(jnp.float32)
+        gap = jnp.full((8, 128), cond_energy[w] - val_energy[v], jnp.float32)
         factor = jnp.sqrt(4.0 / gap) * (1.0 / 512)
+        factor = jnp.concatenate([factor, factor], axis=0)
         same = bra * ket
         cross = bra * pltpu.roll(ket, 64, 1)
         real = same + pltpu.roll(same, 64, 1)
         imag = pltpu.roll(cross, 64, 1) - cross
         return (jnp.where(lane < 64, real, imag) * factor).astype(jnp.bfloat16)
 
-    def pair_copy(k, q):
-        to = lax.rem(c + k, COLS)
-        rows = pl.ds(CHUNK * q, CHUNK)
+    def produce(n, _):
+        turn, first_col = lax.rem(n * 3, CHIPS_Y), (n // CHIPS_Y) * GROUP
+        row = shifted(y, turn, CHIPS_Y) * 2 + core
+        cols = [lax.rem(c + first_col + i, COLS) for i in range(GROUP)]
+        for to in cols:
+            staged[turn, to] = density(row * COLS + to)
+        for i, to in enumerate(cols):
+            copy = remote(
+                staged.at[turn, to], dens.at[c, slab(y)], pair_send.at[turn], pair_recv.at[turn],
+                row=row, col=to,
+            )
+            if i > 0:
+                copy.start()
+            else:
+                @pl.when(n > 0)
+                def _():
+                    copy.start()
+
+                @pl.when(n == 0)
+                def _():
+                    dens[c, slab(y)] = staged[0, c]
+        return 0
+
+    lax.fori_loop(0, CHIPS_Y * COLS // GROUP, produce, 0)
+
+    def pair_group(turn):
+        count = COLS - 1 if isinstance(turn, int) else COLS
         return remote(
-            staged.at[to, rows], dens.at[c, rows], pair_send.at[q, k], pair_recv.at[q, k], col=to
+            staged.at[turn, pl.ds(0, count)],
+            dens.at[pl.ds(0, count), slab(shifted(y, -turn, CHIPS_Y))],
+            pair_send.at[turn], pair_recv.at[turn],
+            row=shifted(y, 1, CHIPS_Y) * 2 + core, col=c,
         )
-
-    def pair_part(q):
-        def step(k, _):
-            to = lax.rem(c + k, COLS)
-            staged[to, pl.ds(CHUNK * q, CHUNK)] = density(to, q)
-            pair_copy(k, q).start()
-            return 0
-
-        lax.fori_loop(1, COLS, step, 0)
-        dens[c, pl.ds(CHUNK * q, CHUNK)] = density(c, q)
-
-    parts = [band_part(q) for q in range(CHUNKS)]
-    parts[0].start()
-    if CHUNKS > 1:
-        parts[1].start()
-    parts[0].middle()
-    for q in range(CHUNKS):
-        if q + 2 < CHUNKS:
-            parts[q + 2].start()
-        if q + 1 < CHUNKS:
-            parts[q + 1].middle()
-        parts[q].end()
-        pair_part(q)
 
     z_tab = z_table[...]
     left_tab = left_table[...]
@@ -237,33 +257,31 @@
             for n in range(len(parts))
         ]
 
-    for q in range(CHUNKS):
-        def arrived(k, _):
-            origin = lax.rem(c - k + COLS, COLS)
-            rows = pl.ds(CHUNK * q, CHUNK)
-            remote(
-                staged.at[origin, rows], dens.at[origin, rows], pair_send.at[q, k], pair_recv.at[q, k],
-                col=origin,
-            ).wait_recv()
-            return 0
-
-        lax.fori_loop(1, COLS, arrived, 0)
-        part = dens[:, pl.ds(CHUNK * q, CHUNK)].reshape(COLS * CHUNK, 128)
+    def along_z(chip):
+        part = dens[:, slab(chip)].reshape(COLS * SLAB, 128)
         got = jnp.dot(
             jnp.concatenate([part, part], axis=1), z_tab, preferred_element_type=jnp.float32
         )
-        first[:, pl.ds(CHUNK * q, CHUNK)] = got.reshape(COLS, CHUNK, 128)
-        if (q + 1) * CHUNK % 64 == 0:
-            plane = (q + 1) * CHUNK // 64 - 1
-
-            def along_y(i, _):
-                got = transform([first[i * 8 + n, pl.ds(64 * plane, 64)] for n in range(8)])
-                for n in range(8):
-                    base = pl.multiple_of((i * 8 + n) * 128 + 64 * plane, 64)
-                    second[pl.ds(base, 64), :] = got[n]
-                return 0
-
-            lax.fori_loop(0, 4, along_y, 0)
+        first[:, slab(chip)] = got.reshape(COLS, SLAB, 128)
+
+    def arrived(turn, _):
+        pair_group(turn).wait_recv()
+        along_z(shifted(y, -turn, CHIPS_Y))
+        return 0
+
+    pair_group(0).wait_recv()
+    along_z(y)
+    lax.fori_loop(1, CHIPS_Y, arrived, 0)
+
+    for plane in range(2):
+        def along_y(i, _):
+            got = transform([first[i * 8 + n, pl.ds(64 * plane, 64)] for n in range(8)])
+            for n in range(8):
+                base = pl.multiple_of((i * 8 + n) * 128 + 64 * plane, 64)
+                second[pl.ds(base, 64), :] = got[n]
+            return 0
+
+        lax.fori_loop(0, 4, along_y, 0)
 
     for i in range(8):
         done = transform([second[pl.ds(i * 8 + n, 64, stride=64), :] for n in range(8)])
@@ -379,15 +397,17 @@
 
     lax.fori_loop(0, COLS, reorder, 0)
 
-    for part in parts:
-        part.finish()
-
-    def pair_end(k, _):
-        for q in range(CHUNKS):
-            pair_copy(k, q).wait_send()
+    for i in range(7):
+        band_push(i).wait_send()
+    for i in range(8):
+        band_mate(i).wait_send()
+
+    def pair_end(turn, _):
+        pair_group(turn).wait_send()
         return 0
 
-    lax.fori_loop(1, COLS, pair_end, 0)
+    pair_group(0).wait_send()
+    lax.fori_loop(1, CHIPS_Y, pair_end, 0)
 
     def amp_end(b, _):
         @pl.when(b // 2 != r)
@@ -421,8 +441,8 @@
         in_specs=[SMEM] * 4 + [VMEM] * 4,
         out_specs=(VMEM, VMEM),
         scratch_shapes=[
-            *[pltpu.VMEM((ROWS, BANDS_DEV, CHUNK, 128), bf16) for _ in range(CHUNKS)],
-            pltpu.VMEM((COLS, 128, 128), bf16),
+            pltpu.VMEM((ROWS, BANDS_DEV, SLAB, 128), bf16),
+            pltpu.VMEM((CHIPS_Y, COLS, SLAB, 128), bf16),
             pltpu.VMEM((COLS, 128, 128), bf16),
             pltpu.VMEM((COLS, 128, 128), f32),
             pltpu.VMEM((4096, 128), f32),
@@ -432,7 +452,7 @@
             pltpu.VMEM((COLS, 8, 128), f32),
             pltpu.VMEM((ROWS, 8, COLS, 128), bf16),
             pltpu.VMEM((4096, 128), f32),
-            dma((CHUNKS, 15)), dma((CHUNKS, 15)), dma((CHUNKS, COLS)), dma((CHUNKS, COLS)),
+            dma((16,)), dma((16,)), dma((CHIPS_Y,)), dma((CHIPS_Y,)),
             dma((COLS,)), dma((2, ROWS)), dma((COLS,)), dma((COLS,)),
             dma((2, 31)), dma((2, 31)), dma((15,)), dma((15,)),
         ],
@@ -443,15 +463,14 @@
     )(val_index, cond_index, val_energy, cond_energy, own, z_table, left_table, index)
 
 
-def product_kernel(real, imag, rhs, out):
-    real = real[...].reshape(512, 128)
-    imag = imag[...].reshape(512, 128)
+def product_kernel(left, rhs, out):
+    j = pl.program_id(0)
+    real = left[j // 4, :, :, j % 4].reshape(512, 128).astype(jnp.float32).T.astype(jnp.bfloat16)
+    imag = left[j // 4, :, :, j % 4 + 4].reshape(512, 128).astype(jnp.float32).T.astype(jnp.bfloat16)
     lhs = jnp.concatenate(
-        [jnp.concatenate([real, imag], axis=0), jnp.concatenate([imag, -real], axis=0)], axis=1
+        [jnp.concatenate([real, imag], axis=1), jnp.concatenate([imag, -real], axis=1)], axis=0
     )
-    got = lax.dot_general(
-        lhs, rhs[...], (((0,), (0,)), ((), ())), preferred_element_type=jnp.float32
-    ) * (-1.0 / 512)
+    got = jnp.dot(lhs, rhs[...], preferred_element_type=jnp.float32) * (-1.0 / 512)
     out[0] = got[:128]
     out[1] = got[128:]
 
@@ -463,14 +482,12 @@
         grid=(8,),
         out_shape=jax.ShapeDtypeStruct((2, 1024, 512), jnp.float32),
         in_specs=[
-            pl.BlockSpec(block, lambda j: (j // 4, 0, 0, j % 4, 0, 0)),
-            pl.BlockSpec(block, lambda j: (j // 4, 0, 0, j % 4 + 4, 0, 0)),
-            VMEM,
+            VMEM, VMEM,
         ],
         out_specs=pl.BlockSpec((2, 128, 512), lambda j: (0, j, 0)),
         compiler_params=pltpu.CompilerParams(vmem_limit_bytes=VMEM_LIMIT),
         name="product",
-    )(left, left, rhs)
+    )(left, rhs)
 
 
 def local(val_waves, cond_waves, val_energy, cond_energy, val_index, cond_index, grid_index):

time: 128 us -> 121 us (0.945)
  Pallas kernels: 124 us -> 118 us
    pallas_call x1, Pallas kernels: 116 us -> 110 us  [window(): pl.pallas_call(window_kernel, out_shape=(jax.ShapeDtypeStruct((2, CHIPS_X...]
where the time goes in v3:
time: 121 us; the launch traced here: 120 us
  Pallas kernels  118 us (98%)
  local copies, waits for them, and re-layouts  1.42 us (1%)
    pallas_call x1, Pallas kernels, window(): pl.pallas_call(window_kernel, out_shape=(jax.ShapeDtypeStruct((2, CHIPS_X...  110 us
    pallas_call x1, Pallas kernels, product(): pl.pallas_call(product_kernel, grid=(8,), out_shape=jax.ShapeDtypeStruct(...  7.59 us

profile of v3, /device:TPU:1, one launch (start us, length us, event | category | flops | bytes accessed | tf_op | source)
XLA Modules:
  0.0 120.4 jit_solution(7059174513730659255)
XLA Ops:
  0.0 1.1 pad_maximum_fusion
  1.1 0.2 reshape.9
  1.4 0.3 copy.12
  1.7 0.8 reshape.10.own
  2.6 110.2 %window.1 = (bf16[2,4,8,8,16,128]{5,4,3,2,1,0:T(8,128)(2,1)}, bf16[1024,512]{1,0:T(8,128)(2,1)}) custom-call(s32[512]{0:T(512)} %val_index.1, s32[512]{0:T(512)} %cond_index.1, f32[16]{0:T(128)} %val_energy.1, f32[64]{0:T(128)} %cond_energy.1, bf16[5,128,128]{2,1,0:T(8,128)(2,1)} %reshape.10.own, bf16[256,128]{1,0:T(8,128)(2,1)} %constant.4.clone.z_table, ...), custom_call_target="tpu_custom_call" | custom-call | tf_op jit(solution)/shard_map/window/pallas_call | solution.py:435
  112.8 7.6 %product.1 = f32[2,1024,512]{2,1,0:T(8,128)} custom-call(bf16[2,4,8,8,16,128]{5,4,3,2,1,0:T(8,128)(2,1)} %get-tuple-element.7.left, bf16[1024,512]{1,0:T(8,128)(2,1)} %get-tuple-element.8.rhs), custom_call_target="tpu_custom_call" | custom-call | tf_op jit(solution)/shard_map/product/pallas_call | solution.py:480

commit v4 on v3

--- a/solution.py
+++ b/solution.py
@@ -379,6 +379,34 @@
         right[r, j] = wide[pl.ds(j, 32, stride=8), :].astype(jnp.bfloat16)
     column = RowGather(lambda slot: right.at[slot], lambda n: right_send.at[n], lambda n: right_recv.at[n])
     column.start()
+
+    for i in range(7):
+        band_push(i).wait_send()
+    for i in range(8):
+        band_mate(i).wait_send()
+
+    def pair_end(turn, _):
+        pair_group(turn).wait_send()
+        return 0
+
+    pair_group(0).wait_send()
+    lax.fori_loop(1, CHIPS_Y, pair_end, 0)
+
+    def amp_end(b, _):
+        @pl.when(b // 2 != r)
+        def _():
+            row_copy(b, b % 2, b // 2).wait_send()
+
+        @pl.when(b != c)
+        def _():
+            col_copy(b).wait_send()
+
+        return 0
+
+    lax.fori_loop(0, COLS, amp_end, 0)
+    early.arrive()
+    early.finish()
+
     for i in range(4):
         late.forward(i)
     column.middle()
@@ -397,33 +425,7 @@
 
     lax.fori_loop(0, COLS, reorder, 0)
 
-    for i in range(7):
-        band_push(i).wait_send()
-    for i in range(8):
-        band_mate(i).wait_send()
-
-    def pair_end(turn, _):
-        pair_group(turn).wait_send()
-        return 0
-
-    pair_group(0).wait_send()
-    lax.fori_loop(1, CHIPS_Y, pair_end, 0)
-
-    def amp_end(b, _):
-        @pl.when(b // 2 != r)
-        def _():
-            row_copy(b, b % 2, b // 2).wait_send()
-
-        @pl.when(b != c)
-        def _():
-            col_copy(b).wait_send()
-
-        return 0
-
-    lax.fori_loop(0, COLS, amp_end, 0)
-    early.arrive()
     late.arrive()
-    early.finish()
     late.finish()
     column.finish()
 

time: 121 us -> 120 us (level)
  no operation moved by 1% of the time
where the time goes in v4:
time: 120 us
  Pallas kernels  117 us (98%)
  local copies, waits for them, and re-layouts  1.42 us (1%)
    pallas_call x1, Pallas kernels, window(): pl.pallas_call(window_kernel, out_shape=(jax.ShapeDtypeStruct((2, CHIPS_X...  110 us
    pallas_call x1, Pallas kernels, product(): pl.pallas_call(product_kernel, grid=(8,), out_shape=jax.ShapeDtypeStruct(...  7.58 us

profile of v4, /device:TPU:1, one launch (start us, length us, event | category | flops | bytes accessed | tf_op | source)
XLA Modules:
  0.0 119.7 jit_solution(5391139487818770420)
XLA Ops:
  0.0 1.1 pad_maximum_fusion
  1.1 0.2 reshape.9
  1.4 0.3 copy.12
  1.7 0.8 reshape.10.own
  2.6 109.5 %window.1 = (bf16[2,4,8,8,16,128]{5,4,3,2,1,0:T(8,128)(2,1)}, bf16[1024,512]{1,0:T(8,128)(2,1)}) custom-call(s32[512]{0:T(512)} %val_index.1, s32[512]{0:T(512)} %cond_index.1, f32[16]{0:T(128)} %val_energy.1, f32[64]{0:T(128)} %cond_energy.1, bf16[5,128,128]{2,1,0:T(8,128)(2,1)} %reshape.10.own, bf16[256,128]{1,0:T(8,128)(2,1)} %constant.4.clone.z_table, ...), custom_call_target="tpu_custom_call" | custom-call | tf_op jit(solution)/shard_map/window/pallas_call | solution.py:437
  112.1 7.6 %product.1 = f32[2,1024,512]{2,1,0:T(8,128)} custom-call(bf16[2,4,8,8,16,128]{5,4,3,2,1,0:T(8,128)(2,1)} %get-tuple-element.7.left, bf16[1024,512]{1,0:T(8,128)(2,1)} %get-tuple-element.8.rhs), custom_call_target="tpu_custom_call" | custom-call | tf_op jit(solution)/shard_map/product/pallas_call | solution.py:482
